TPU v7x, 32 devices: a whole 2x2x4 slice. The times are simulated.
32 devices in a mesh: groups: 2 (over y), atoms: 16 (over z, x, core).
Axes of the slice: x: 2, y: 2, z: 4, core: 2. Of those that a mesh axis runs over, the one named last changes fastest.
Arguments:
- particle_coordinates: float32 [3, 4096], P(None, ('groups', 'atoms')), parts along dimension 1, may hold values from 0 to 72
- integer_lattice_modes: int32 [3, 4096], replicated, may hold values from -6 to 6
- hidden_embeddings: bfloat16 [2, 4096, 128], P(None, ('groups', 'atoms')), parts along dimension 1, may hold values from -6 to 6
- cached_density_modes: bfloat16 [4, 4096, 256], P('groups'), parts along dimension 0, may hold values from -6 to 6
- spectral_kernels: bfloat16 [2, 4096, 128], replicated, may hold values from -4 to 4
- final_embedding_adjoint: bfloat16 [4096, 128], P(('groups', 'atoms')), parts along dimension 0, may hold values from -6 to 6
- particle_result_line: int32 [4096], P(('groups', 'atoms')), parts along dimension 0, may hold values from 0 to 2047, as said below
Outputs:
- feat_grad: float32 [4096, 128], P(('groups', 'atoms')), parts along dimension 0
- pos_grad: float32 [3, 4096], P(None, ('groups', 'atoms')), parts along dimension 1
- filter_grad: float32 [2, 8192, 128], P(None, ('groups', 'atoms')), parts along dimension 1
There are 2 independent parts, one for each index of `groups`. A program takes and returns all parts, laid end to end along the dimension named above; an argument that names none is the same for every part. Nothing has to cross between parts.
Inputs may be any that keep to these rules, and one draw needn't show every extreme that they name: `particle_result_line`: a permutation of the atoms; the atoms of each aligned block of 128 rows send exactly the same number of atoms to every aligned block of 128 output rows.
All inputs are finite; a program needn't handle non-finite values.
Results may differ from a plain program's by a relative error of at most 0.0075.
Values may be sent and summed in bfloat16 or wider, within the bound.
A program may use at most 128 MiB of HBM per device.

v0:
```python
import functools
import math

import jax
import jax.numpy as jnp
from jax import lax
from jax.experimental import pallas as pl
from jax.experimental.pallas import tpu as pltpu
from jax.sharding import PartitionSpec as P

BOX = 72
AXIS = "atoms"
F32, BF16 = jnp.float32, jnp.bfloat16
COS_TERMS = (0.999999212, -19.7389804, 64.9286585, -85.2716283, 58.7905066, -21.0711085)
SIN_TERMS = (6.28318492, -41.3415893, 81.5999439, -76.6144759, 41.3428894, -12.4712447)


def trig_of_turns(turns):
    part = turns - jnp.round(turns)
    square = part * part
    cos = COS_TERMS[-1]
    sin = SIN_TERMS[-1]
    for a in COS_TERMS[-2::-1]:
        cos = cos * square + a
    for a in SIN_TERMS[-2::-1]:
        sin = sin * square + a
    return cos.astype(BF16), (sin * part).astype(BF16)


def dot(a, b, ca=1, cb=0):
    return lax.dot_general(a, b, (((ca,), (cb,)), ((), ())), preferred_element_type=F32)


def repeat(count, step, most=8):
    if count <= most:
        for i in range(count):
            step(i)
    else:

        def run(i, carry):
            step(i)
            return carry

        lax.fori_loop(0, count, run, 0)


def pieces_of(rows):
    keep = lax.broadcasted_iota(jnp.int32, rows.shape, 0) < 3
    value = jnp.where(keep, rows * (1.0 / BOX), 0.0)
    high = value.astype(BF16).astype(F32)
    rest = value - high
    mid = rest.astype(BF16).astype(F32)
    return jnp.concatenate([high, mid, rest - mid, jnp.zeros_like(rows)], axis=0).astype(BF16)


def kernel(
    dims,
    coords_ref,
    modes_ref,
    hidden_ref,
    density_hbm,
    filter_hbm,
    cot_ref,
    line_ref,
    feat_ref,
    pos_ref,
    grad_ref,
    density,
    filters,
    meta,
    lattice,
    window,
    trig,
    wide,
    weights,
    fin,
    choose,
    message,
    slope,
    cot,
    partial,
    pos_sum,
    acc,
    s1,
    r1,
    s2,
    r2,
    s3,
    r3,
    load_sem,
    meta_send,
    meta_recv,
    hid_send,
    hid_recv,
    gat_send,
    gat_recv,
    s1_send,
    s1_recv,
    s2_send,
    s2_recv,
    s3_send,
    s3_recv,
):
    Z, X = dims
    n = Z * X * 2
    ch = cot_ref.shape[1]
    A = cot_ref.shape[0]
    modes = modes_ref.shape[1]
    own = modes // n
    atoms = n * A
    k_scale = modes ** (-0.5)
    a_scale = atoms ** (-0.5)
    me = lax.axis_index(AXIS)
    c = lax.rem(me, 2)
    x = lax.rem(me // 2, X)
    z = me // (2 * X)
    chunks = load_sem.shape[0]
    step_modes = modes // chunks

    def dev(zz, xx, cc):
        return (zz * X + xx) * 2 + cc

    def up(base, j, size):
        return lax.rem(base + j, size)

    def cols(d):
        return pl.ds(pl.multiple_of(d * A, A), A)

    def remote(src, dst, ssem, rsem, peer):
        return pltpu.make_async_remote_copy(
            src_ref=src,
            dst_ref=dst,
            send_sem=ssem,
            recv_sem=rsem,
            device_id={AXIS: peer},
            device_id_type=pl.DeviceIdType.MESH,
        )

    def loads(q):
        part = pl.ds(pl.multiple_of(q * step_modes, step_modes), step_modes)
        return (
            pltpu.make_async_copy(density_hbm.at[:, part], density.at[:, part], load_sem.at[q, 0]),
            pltpu.make_async_copy(filter_hbm.at[:, part], filters.at[:, part], load_sem.at[q, 1]),
        )

    def start_load(q):
        for copy in loads(q):
            copy.start()

    repeat(chunks, start_load)

    barrier = pltpu.get_barrier_semaphore()

    def greet(j):
        pl.semaphore_signal(
            barrier,
            inc=1,
            device_id={AXIS: up(me, j + 1, n)},
            device_id_type=pl.DeviceIdType.MESH,
        )

    repeat(n - 1, greet, 15)

    mine = cols(me)
    meta[:, mine] = jnp.zeros((8, A), F32)
    meta[0:3, mine] = coords_ref[...]
    meta[3:4, mine] = line_ref[...].astype(F32)
    for b in range(2):
        wide[b, ch : 2 * ch, mine] = hidden_ref[b].astype(F32).T.astype(BF16)
    pl.semaphore_wait(barrier, n - 1)

    def meta_copy(j):
        peer = up(me, j + 1, n)
        return remote(
            meta.at[:, mine], meta.at[:, mine], meta_send.at[j], meta_recv.at[j], peer
        )

    repeat(n - 1, lambda j: meta_copy(j).start(), 15)

    class Gather:
        def __init__(self, view, send, recv):
            self.view, self.send, self.recv = view, send, recv

        def copy(self, d, peer, k):
            return remote(self.view(d), self.view(d), self.send.at[k], self.recv.at[d], peer)

        def arrive(self, d):
            self.copy(d, up(me, 1, n), 0).wait_recv()

        def spread(self, d, j):
            for i in range(1, X):
                self.copy(d, dev(z, up(x, i, X), c), Z - 1 + j * (X - 1) + i - 1).start()
            self.copy(d, dev(z, x, 1 - c), Z - 1 + Z * (X - 1) + j * X).start()

        def start(self):
            repeat(
                Z - 1, lambda j: self.copy(me, dev(up(z, j + 1, Z), x, c), j).start()
            )
            self.spread(me, 0)

        def along_x(self):
            def step(j):
                d = dev(up(z, j + 1, Z), x, c)
                self.arrive(d)
                self.spread(d, j + 1)

            repeat(Z - 1, step)

        def along_core(self):
            def step(j):
                for i in range(1, X):
                    d = dev(up(z, j, Z), up(x, i, X), c)
                    self.arrive(d)
                    self.copy(d, dev(z, x, 1 - c), Z - 1 + Z * (X - 1) + j * X + i).start()

            repeat(Z, step)

        def finish(self):
            def step(j):
                for i in range(X):
                    self.arrive(dev(up(z, j, Z), up(x, i, X), 1 - c))

            repeat(Z, step)
            repeat(n - 1, lambda k: self.copy(me, up(me, 1, n), k).wait_send(), 15)

    hidden = Gather(lambda d: wide.at[:, pl.ds(ch, ch), cols(d)], hid_send, hid_recv)
    grads = [
        Gather(lambda d, b=b: wide.at[b, pl.ds(0, ch), cols(d)], gat_send, gat_recv)
        for b in range(2)
    ]
    final = Gather(lambda d: fin.at[:, cols(d)], gat_send, gat_recv)
    hidden.start()

    eight = jnp.concatenate(
        [modes_ref[...].astype(F32), jnp.zeros((5, modes), F32)], axis=0
    )
    lattice[...] = jnp.concatenate([eight, eight, eight, jnp.zeros_like(eight)], axis=0)
    my_pieces = pieces_of(meta[:, mine])
    message[...] = jnp.zeros_like(message)

    def message_step(q):
        part = pl.ds(pl.multiple_of(q * step_modes, step_modes), step_modes)
        cos, sin = trig_of_turns(dot(my_pieces, lattice[:, part].astype(BF16), 0, 0))
        for copy in loads(q):
            copy.wait()
        even, odd = [], []
        for b in range(2):
            factor = filters[b, part, :]
            even.append(density[b, part, 0:ch] * factor)
            odd.append(density[b, part, ch : 2 * ch] * factor)
        message[...] += dot(cos, jnp.concatenate(even, axis=1)) + dot(
            sin, jnp.concatenate(odd, axis=1)
        )

    repeat(chunks, message_step, 0)

    for b in range(2):
        value = k_scale * message[:, b * ch : (b + 1) * ch]
        logistic = 1.0 / (1.0 + jnp.exp(-value))
        slope[b] = (logistic * (1.0 + value * (1.0 - logistic))).T
    cot[...] = cot_ref[...].astype(F32).T
    wide[1, 0:ch, mine] = (cot[...] * slope[1]).astype(BF16)
    grads[1].start()
    hidden.along_x()

    repeat(n - 1, lambda j: meta_copy(j).wait_recv(), 15)
    width = window.shape[0]
    base = (me * own) // width * width
    near = lattice[:, pl.ds(pl.multiple_of(base, width), width)]
    window[...] = jnp.concatenate([near, jnp.zeros((96, width), F32)], axis=0).T
    own_modes = window[pl.ds(pl.multiple_of(me * own - base, own), own), :].astype(BF16)
    tile = 2 * A

    def trig_step(q):
        part = pl.ds(pl.multiple_of(q * tile, tile), tile)
        turns = dot(own_modes[:, 0:32], pieces_of(meta[:, part]))
        cos, sin = trig_of_turns(turns)
        trig[0:own, part] = cos
        trig[own : 2 * own, part] = sin
        rows = lax.broadcasted_iota(jnp.int32, (A, tile), 0) + me * A
        hit = meta[3:4, part] == rows.astype(F32)
        choose[:, part] = jnp.where(hit, 1.0, 0.0).astype(BF16)

    def trig_range(lo, hi):
        def run(q, carry):
            trig_step(q)
            return carry

        lax.fori_loop(lo, hi, run, 0)

    tiles = atoms // tile
    trig_range(0, tiles // 2)
    grads[1].along_x()
    hidden.along_core()
    trig_range(tiles // 2, tiles * 3 // 4)
    grads[1].along_core()
    trig_range(tiles * 3 // 4, tiles)
    grads[1].finish()

    group = 2 * X * A
    my_rows = pl.ds(pl.multiple_of(me * own, own), own)

    def adjoints(b):
        adjoint = k_scale * dot(trig[...], wide[b, 0:ch, :], 1, 1)
        even, odd = adjoint[0:own], adjoint[own:]
        saved = density[b, my_rows, :].astype(F32)
        factor = filters[b, my_rows, :].astype(F32)
        grad_ref[b] = even * saved[:, 0:ch] + odd * saved[:, ch:]
        ratio = k_scale / a_scale
        weights[0:own, 0:ch] = (saved[:, 0:ch] * factor * ratio).astype(BF16)
        weights[own:, 0:ch] = (saved[:, ch:] * factor * ratio).astype(BF16)
        both = jnp.concatenate([even * factor, odd * factor], axis=0)
        weights[:, ch:] = both.astype(BF16)
        return both.T.astype(BF16)

    def pos_group(b, zt):
        for h in range(X):
            part = pl.ds(pl.multiple_of(zt * group + h * tile, tile), tile)
            mix = dot(weights[...], wide[b, :, part])
            slant = (
                trig[0:own, part].astype(F32) * mix[own:]
                - trig[own:, part].astype(F32) * mix[0:own]
            )
            add = dot(own_modes[:, 0:16], slant.astype(BF16), 0, 0)
            if b == 1:
                pos_sum[:, part] = add
            else:
                pos_sum[:, part] += add

    def order(k):
        return up(z, k + 1, Z)

    def first_copy(zt, rows):
        return remote(
            s1.at[zt, pl.ds(0, rows)],
            r1.at[zt, pl.ds(0, rows)],
            s1_send.at[zt],
            s1_recv.at[zt],
            dev(z, x, 1 - c),
        )

    def second_copy(zt, i, rows):
        k = zt * (X - 1) + i - 1
        return remote(
            s2.at[k, pl.ds(0, rows)],
            r2.at[k, pl.ds(0, rows)],
            s2_send.at[k],
            s2_recv.at[k],
            dev(z, up(x, i, X), c),
        )

    def third_copy(k, rows):
        return remote(
            s3.at[k, pl.ds(0, rows)],
            r3.at[k, pl.ds(0, rows)],
            s3_send.at[k],
            s3_recv.at[k],
            dev(order(k), x, c),
        )

    def block(b, rows):
        turned = adjoints(b)

        def one(k):
            zt = order(k)
            part = pl.ds(pl.multiple_of(zt * group, group), group)
            partial[zt, 0:ch, :] = a_scale * dot(turned, trig[:, part])
            if rows > ch:
                pos_group(b, zt)
                partial[zt, ch:rows, :] = (a_scale * 2.0 * math.pi / BOX) * pos_sum[:, part]
            for i in range(X):
                s1[zt, 0:rows, i * A : (i + 1) * A] = partial[
                    zt, 0:rows, cols(2 * i + 1 - c)
                ].astype(BF16)
            first_copy(zt, rows).start()

        def two(k):
            zt = order(k)
            first_copy(zt, rows).wait_recv()
            for i in range(1, X):
                xt = up(x, i, X)
                s2[zt * (X - 1) + i - 1, 0:rows, :] = (
                    partial[zt, 0:rows, cols(2 * xt + c)]
                    + r1[zt, 0:rows, cols(xt)].astype(F32)
                ).astype(BF16)
                second_copy(zt, i, rows).start()
            acc[zt, 0:rows, :] = partial[zt, 0:rows, cols(2 * x + c)] + r1[
                zt, 0:rows, cols(x)
            ].astype(F32)

        def summed(k):
            zt = order(k)
            total = acc[zt, 0:rows, :]
            for i in range(1, X):
                second_copy(zt, i, rows).wait_recv()
                total = total + r2[zt * (X - 1) + i - 1, 0:rows, :].astype(F32)
            return total

        def three(k):
            s3[k, 0:rows, :] = summed(k).astype(BF16)
            third_copy(k, rows).start()

        repeat(Z, one, 4)
        if rows == ch:
            for k in range(min(2, Z)):
                pos_group(b, order(k))
        repeat(Z, two, 4)
        repeat(Z - 1, three, 4)
        acc[z, 0:rows, :] = summed(Z - 1)

        def last(k):
            third_copy(k, rows).wait_recv()
            acc[z, 0:rows, :] += r3[k, 0:rows, :].astype(F32)

        repeat(Z - 1, last, 4)

        def sent(k):
            first_copy(k, rows).wait_send()
            for i in range(1, X):
                second_copy(k, i, rows).wait_send()

        repeat(Z, sent, 4)
        repeat(Z - 1, lambda k: third_copy(k, rows).wait_send(), 4)

    hidden.finish()
    block(1, ch)
    cot[...] += acc[z, 0:ch, :]
    wide[0, 0:ch, mine] = (cot[...] * slope[0]).astype(BF16)
    grads[0].start()
    repeat(max(Z - 2, 0), lambda k: pos_group(1, order(k + 2)), 4)
    grads[0].along_x()
    grads[0].along_core()
    grads[0].finish()
    block(0, ch + 16)
    fin[0:ch, mine] = (cot[...] + acc[z, 0:ch, :]).astype(BF16)
    fin[ch:, mine] = acc[z, ch:, :].astype(BF16)
    final.start()
    final.along_x()
    final.along_core()
    final.finish()
    feat_ref[...] = dot(choose[...], fin[0:ch, :], 1, 1)
    pos_ref[...] = dot(fin[ch:, :], choose[...], 1, 1)[0:3]
    repeat(n - 1, lambda j: meta_copy(j).wait_send(), 15)


def body(
    dims,
    particle_coordinates,
    integer_lattice_modes,
    hidden_embeddings,
    cached_density_modes,
    spectral_kernels,
    final_embedding_adjoint,
    particle_result_line,
):
    Z, X = dims
    n = Z * X * 2
    blocks, A, ch = hidden_embeddings.shape
    modes = integer_lattice_modes.shape[1]
    own = modes // n
    atoms = n * A
    rows = ch + 16
    chunks = 8
    vmem = pl.BlockSpec(memory_space=pltpu.VMEM)
    hbm = pl.BlockSpec(memory_space=pl.ANY)
    dma = pltpu.SemaphoreType.DMA
    scratch = [
        pltpu.VMEM((blocks, modes, 2 * ch), BF16),
        pltpu.VMEM((blocks, modes, ch), BF16),
        pltpu.VMEM((8, atoms), F32),
        pltpu.VMEM((32, modes), F32),
        pltpu.VMEM((max(own, 128), 128), F32),
        pltpu.VMEM((2 * own, atoms), BF16),
        pltpu.VMEM((blocks, 2 * ch, atoms), BF16),
        pltpu.VMEM((2 * own, 2 * ch), BF16),
        pltpu.VMEM((rows, atoms), BF16),
        pltpu.VMEM((A, atoms), BF16),
        pltpu.VMEM((A, blocks * ch), F32),
        pltpu.VMEM((blocks, ch, A), F32),
        pltpu.VMEM((ch, A), F32),
        pltpu.VMEM((Z, rows, 2 * X * A), F32),
        pltpu.VMEM((16, atoms), F32),
        pltpu.VMEM((Z, rows, A), F32),
        pltpu.VMEM((Z, rows, X * A), BF16),
        pltpu.VMEM((Z, rows, X * A), BF16),
        pltpu.VMEM((Z * (X - 1), rows, A), BF16),
        pltpu.VMEM((Z * (X - 1), rows, A), BF16),
        pltpu.VMEM((Z - 1, rows, A), BF16),
        pltpu.VMEM((Z - 1, rows, A), BF16),
        dma((chunks, 2)),
        dma((n - 1,)),
        dma((n - 1,)),
        dma((n - 1,)),
        dma((n,)),
        dma((n - 1,)),
        dma((n,)),
        dma((Z,)),
        dma((Z,)),
        dma((Z * (X - 1),)),
        dma((Z * (X - 1),)),
        dma((Z - 1,)),
        dma((Z - 1,)),
    ]
    return pl.pallas_call(
        functools.partial(kernel, dims),
        out_shape=(
            jax.ShapeDtypeStruct((A, ch), F32),
            jax.ShapeDtypeStruct((3, A), F32),
            jax.ShapeDtypeStruct((blocks, own, ch), F32),
        ),
        in_specs=[vmem, vmem, vmem, hbm, hbm, vmem, vmem],
        out_specs=(vmem, vmem, vmem),
        scratch_shapes=scratch,
        compiler_params=pltpu.CompilerParams(
            collective_id=0, has_side_effects=True, vmem_limit_bytes=60 * 1024 * 1024
        ),
    )(
        particle_coordinates,
        integer_lattice_modes,
        hidden_embeddings,
        cached_density_modes,
        spectral_kernels,
        final_embedding_adjoint,
        particle_result_line.reshape(1, A),
    )


def chip_grid(mesh):
    chips = mesh.shape[AXIS] // 2
    first = mesh.devices[0]
    inner = 0
    try:
        inner = len({device.coords[0] for device in first})
    except AttributeError:
        pass
    if inner < 2 or chips % inner or chips // inner < 2:
        inner = 2
    return chips // inner, inner


def solution(mesh):
    in_specs = (
        P(None, ("groups", "atoms")),
        P(),
        P(None, ("groups", "atoms"), None),
        P("groups", None, None),
        P(),
        P(("groups", "atoms"), None),
        P(("groups", "atoms")),
    )
    out_specs = (
        P(("groups", "atoms"), None),
        P(None, ("groups", "atoms")),
        P(None, ("groups", "atoms"), None),
    )
    return jax.shard_map(
        functools.partial(body, chip_grid(mesh)),
        mesh=mesh,
        in_specs=in_specs,
        out_specs=out_specs,
        check_vma=False,
    )
```

profile of v0, /device:TPU:0, one launch (start us, length us, event | category | flops | bytes accessed | tf_op | source)
XLA Modules:
  0.0 73.7 jit_solution(3163191112910912489)
XLA Ops:
  0.6 68.7 %shard_map.94 = (f32[128,128]{1,0:T(8,128)}, f32[3,128]{1,0:T(4,128)}, f32[2,256,128]{2,1,0:T(8,128)}) custom-call(f32[3,128]{1,0:T(4,128)} %coords_ref.1, s32[3,4096]{1,0:T(4,128)} %modes_ref.1, bf16[2,128,128]{2,1,0:T(8,128)(2,1)} %hidden_ref.1, bf16[2,4096,256]{2,1,0:T(8,128)(2,1)} %density_hbm.1, bf16[2,4096,128]{2,1,0:T(8,128)(2,1)} %filter_hbm.1, ...), custom_call_target="tpu_custom_call" | custom-call | tf_op jit(solution)/shard_map/pallas_call | solution.py:504
  69.3 1.5 %copy.13 = f32[128,128]{1,0:T(8,128)} copy(f32[128,128]{1,0:T(8,128)} %get-tuple-element.6) | data formatting | bytes 131072
  70.8 1.3 %copy.14 = f32[3,128]{1,0:T(4,128)} copy(f32[3,128]{1,0:T(4,128)} %get-tuple-element.7) | data formatting | bytes 3072
  72.0 1.7 %copy.15 = f32[2,256,128]{2,1,0:T(8,128)} copy(f32[2,256,128]{2,1,0:T(8,128)} %get-tuple-element.8) | data formatting | bytes 524288
where the time goes:
time: 74 us; the launch traced here: 73.7 us
  Pallas kernels  68.7 us (93%)
  local copies, waits for them, and re-layouts  4.4 us (6%)
    pallas_call x1, Pallas kernels, body(): pl.pallas_call(functools.partial(kernel, dims), out_shape=(jax.ShapeDtype...  68.7 us
    unnamed x3, local copies, waits for them, and re-layouts  4.4 us

commit v1 on v0

--- a/solution.py
+++ b/solution.py
@@ -261,7 +261,6 @@
     cot[...] = cot_ref[...].astype(F32).T
     wide[1, 0:ch, mine] = (cot[...] * slope[1]).astype(BF16)
     grads[1].start()
-    hidden.along_x()
 
     repeat(n - 1, lambda j: meta_copy(j).wait_recv(), 15)
     width = window.shape[0]
@@ -291,7 +290,7 @@
     tiles = atoms // tile
     trig_range(0, tiles // 2)
     grads[1].along_x()
-    hidden.along_core()
+    hidden.along_x()
     trig_range(tiles // 2, tiles * 3 // 4)
     grads[1].along_core()
     trig_range(tiles * 3 // 4, tiles)
@@ -402,8 +401,7 @@
 
         repeat(Z, one, 4)
         if rows == ch:
-            for k in range(min(2, Z)):
-                pos_group(b, order(k))
+            hidden.along_core()
         repeat(Z, two, 4)
         repeat(Z - 1, three, 4)
         acc[z, 0:rows, :] = summed(Z - 1)
@@ -422,12 +420,12 @@
         repeat(Z, sent, 4)
         repeat(Z - 1, lambda k: third_copy(k, rows).wait_send(), 4)
 
-    hidden.finish()
     block(1, ch)
     cot[...] += acc[z, 0:ch, :]
     wide[0, 0:ch, mine] = (cot[...] * slope[0]).astype(BF16)
     grads[0].start()
-    repeat(max(Z - 2, 0), lambda k: pos_group(1, order(k + 2)), 4)
+    hidden.finish()
+    repeat(Z, lambda k: pos_group(1, order(k)), 4)
     grads[0].along_x()
     grads[0].along_core()
     grads[0].finish()

time: 74 us -> 70.2 us (0.949)
  Pallas kernels: 68.7 us -> 64.9 us
    pallas_call x1, Pallas kernels: 68.7 us -> 64.9 us  [body(): pl.pallas_call(functools.partial(kernel, dims), out_shape=(jax.ShapeDtype...]
where the time goes in v1:
time: 70.2 us; the launch traced here: 69.9 us
  Pallas kernels  64.9 us (92%)
  local copies, waits for them, and re-layouts  4.4 us (6%)
    pallas_call x1, Pallas kernels, body(): pl.pallas_call(functools.partial(kernel, dims), out_shape=(jax.ShapeDtype...  64.9 us
    unnamed x3, local copies, waits for them, and re-layouts  4.4 us

profile of v1, /device:TPU:0, one launch (start us, length us, event | category | flops | bytes accessed | tf_op | source)
XLA Modules:
  0.0 69.9 jit_solution(9068400967798441890)
XLA Ops:
  0.6 64.9 %shard_map.94 = (f32[128,128]{1,0:T(8,128)}, f32[3,128]{1,0:T(4,128)}, f32[2,256,128]{2,1,0:T(8,128)}) custom-call(f32[3,128]{1,0:T(4,128)} %coords_ref.1, s32[3,4096]{1,0:T(4,128)} %modes_ref.1, bf16[2,128,128]{2,1,0:T(8,128)(2,1)} %hidden_ref.1, bf16[2,4096,256]{2,1,0:T(8,128)(2,1)} %density_hbm.1, bf16[2,4096,128]{2,1,0:T(8,128)(2,1)} %filter_hbm.1, ...), custom_call_target="tpu_custom_call" | custom-call | tf_op jit(solution)/shard_map/pallas_call | solution.py:502
  65.5 1.5 %copy.13 = f32[128,128]{1,0:T(8,128)} copy(f32[128,128]{1,0:T(8,128)} %get-tuple-element.6) | data formatting | bytes 131072
  67.0 1.3 %copy.14 = f32[3,128]{1,0:T(4,128)} copy(f32[3,128]{1,0:T(4,128)} %get-tuple-element.7) | data formatting | bytes 3072
  68.3 1.7 %copy.15 = f32[2,256,128]{2,1,0:T(8,128)} copy(f32[2,256,128]{2,1,0:T(8,128)} %get-tuple-element.8) | data formatting | bytes 524288

commit v2 on v1

--- a/solution.py
+++ b/solution.py
@@ -123,6 +123,15 @@
     def up(base, j, size):
         return lax.rem(base + j, size)
 
+    def swap(j):
+        if Z & (Z - 1):
+            return up(z, j, Z)
+        total, bit = 0, 1
+        while bit < Z:
+            total = total + bit * lax.rem(lax.div(z, bit) + (j // bit) % 2, 2)
+            bit *= 2
+        return total
+
     def cols(d):
         return pl.ds(pl.multiple_of(d * A, A), A)
 
@@ -194,13 +203,13 @@
 
         def start(self):
             repeat(
-                Z - 1, lambda j: self.copy(me, dev(up(z, j + 1, Z), x, c), j).start()
+                Z - 1, lambda j: self.copy(me, dev(swap(j + 1), x, c), j).start()
             )
             self.spread(me, 0)
 
         def along_x(self):
             def step(j):
-                d = dev(up(z, j + 1, Z), x, c)
+                d = dev(swap(j + 1), x, c)
                 self.arrive(d)
                 self.spread(d, j + 1)
 
@@ -209,7 +218,7 @@
         def along_core(self):
             def step(j):
                 for i in range(1, X):
-                    d = dev(up(z, j, Z), up(x, i, X), c)
+                    d = dev(swap(j), up(x, i, X), c)
                     self.arrive(d)
                     self.copy(d, dev(z, x, 1 - c), Z - 1 + Z * (X - 1) + j * X + i).start()
 
@@ -218,7 +227,7 @@
         def finish(self):
             def step(j):
                 for i in range(X):
-                    self.arrive(dev(up(z, j, Z), up(x, i, X), 1 - c))
+                    self.arrive(dev(swap(j), up(x, i, X), 1 - c))
 
             repeat(Z, step)
             repeat(n - 1, lambda k: self.copy(me, up(me, 1, n), k).wait_send(), 15)
@@ -327,7 +336,7 @@
                 pos_sum[:, part] += add
 
     def order(k):
-        return up(z, k + 1, Z)
+        return up(z, k + 1, Z) if Z & (Z - 1) else swap(Z - 1 - k)
 
     def first_copy(zt, rows):
         return remote(

time: 70.2 us -> 70.3 us (level)
  no operation moved by 1% of the time
where the time goes in v2:
time: 70.3 us; the launch traced here: 70 us
  Pallas kernels  65 us (92%)
  local copies, waits for them, and re-layouts  4.4 us (6%)
    pallas_call x1, Pallas kernels, body(): pl.pallas_call(functools.partial(kernel, dims), out_shape=(jax.ShapeDtype...  65 us
    unnamed x3, local copies, waits for them, and re-layouts  4.4 us

profile of v2, /device:TPU:0, one launch (start us, length us, event | category | flops | bytes accessed | tf_op | source)
XLA Modules:
  0.0 70.0 jit_solution(1762126092974254378)
XLA Ops:
  0.6 65.0 %shard_map.94 = (f32[128,128]{1,0:T(8,128)}, f32[3,128]{1,0:T(4,128)}, f32[2,256,128]{2,1,0:T(8,128)}) custom-call(f32[3,128]{1,0:T(4,128)} %coords_ref.1, s32[3,4096]{1,0:T(4,128)} %modes_ref.1, bf16[2,128,128]{2,1,0:T(8,128)(2,1)} %hidden_ref.1, bf16[2,4096,256]{2,1,0:T(8,128)(2,1)} %density_hbm.1, bf16[2,4096,128]{2,1,0:T(8,128)(2,1)} %filter_hbm.1, ...), custom_call_target="tpu_custom_call" | custom-call | tf_op jit(solution)/shard_map/pallas_call | solution.py:511
  65.6 1.5 %copy.13 = f32[128,128]{1,0:T(8,128)} copy(f32[128,128]{1,0:T(8,128)} %get-tuple-element.6) | data formatting | bytes 131072
  67.1 1.3 %copy.14 = f32[3,128]{1,0:T(4,128)} copy(f32[3,128]{1,0:T(4,128)} %get-tuple-element.7) | data formatting | bytes 3072
  68.4 1.7 %copy.15 = f32[2,256,128]{2,1,0:T(8,128)} copy(f32[2,256,128]{2,1,0:T(8,128)} %get-tuple-element.8) | data formatting | bytes 524288

commit v3 on v2

--- a/solution.py
+++ b/solution.py
@@ -411,8 +411,13 @@
         repeat(Z, one, 4)
         if rows == ch:
             hidden.along_core()
-        repeat(Z, two, 4)
-        repeat(Z - 1, three, 4)
+        two(0)
+
+        def both(k):
+            two(k + 1)
+            three(k)
+
+        repeat(Z - 1, both, 4)
         acc[z, 0:rows, :] = summed(Z - 1)
 
         def last(k):

time: 70.3 us -> 72.3 us (1.028)
  Pallas kernels: 65 us -> 67 us
    pallas_call x1, Pallas kernels: 65 us -> 67 us  [body(): pl.pallas_call(functools.partial(kernel, dims), out_shape=(jax.ShapeDtype...]
where the time goes in v3:
time: 72.3 us; the launch traced here: 72.1 us
  Pallas kernels  67 us (93%)
  local copies, waits for them, and re-layouts  4.4 us (6%)
    pallas_call x1, Pallas kernels, body(): pl.pallas_call(functools.partial(kernel, dims), out_shape=(jax.ShapeDtype...  67 us
    unnamed x3, local copies, waits for them, and re-layouts  4.4 us

profile of v3, /device:TPU:0, one launch (start us, length us, event | category | flops | bytes accessed | tf_op | source)
XLA Modules:
  0.0 72.1 jit_solution(16038403721242465593)
XLA Ops:
  0.6 67.0 %shard_map.94 = (f32[128,128]{1,0:T(8,128)}, f32[3,128]{1,0:T(4,128)}, f32[2,256,128]{2,1,0:T(8,128)}) custom-call(f32[3,128]{1,0:T(4,128)} %coords_ref.1, s32[3,4096]{1,0:T(4,128)} %modes_ref.1, bf16[2,128,128]{2,1,0:T(8,128)(2,1)} %hidden_ref.1, bf16[2,4096,256]{2,1,0:T(8,128)(2,1)} %density_hbm.1, bf16[2,4096,128]{2,1,0:T(8,128)(2,1)} %filter_hbm.1, ...), custom_call_target="tpu_custom_call" | custom-call | tf_op jit(solution)/shard_map/pallas_call | solution.py:516
  67.7 1.5 %copy.13 = f32[128,128]{1,0:T(8,128)} copy(f32[128,128]{1,0:T(8,128)} %get-tuple-element.6) | data formatting | bytes 131072
  69.2 1.3 %copy.14 = f32[3,128]{1,0:T(4,128)} copy(f32[3,128]{1,0:T(4,128)} %get-tuple-element.7) | data formatting | bytes 3072
  70.4 1.7 %copy.15 = f32[2,256,128]{2,1,0:T(8,128)} copy(f32[2,256,128]{2,1,0:T(8,128)} %get-tuple-element.8) | data formatting | bytes 524288
